TPU v7x, 32 devices: a whole 2x2x4 slice. The times are simulated.
32 devices in a mesh: seq: 16 (over z, y, core), hid: 2 (over x).
Axes of the slice: x: 2, y: 2, z: 4, core: 2. Of those that a mesh axis runs over, the one named last changes fastest.
Arguments:
- queries: bfloat16 [6144, 3072], P('seq', 'hid'), may hold values from -6 to 6
- keys: bfloat16 [6144, 3072], P('seq', 'hid'), may hold values from -4 to 4
- values: bfloat16 [6144, 3072], P('seq', 'hid'), may hold values from -6 to 6
- residual: bfloat16 [6144, 3072], P('seq', 'hid'), may hold values from -24 to 24
- w_in: bfloat16 [3072, 6144], P(None, 'hid'), may hold values from -0.109375 to 0.109375
- w_out: bfloat16 [6144, 3072], P('hid', 'seq'), may hold values from -0.078125 to 0.078125
- mod_scale: float32 [3072], replicated, may hold values from -0.5 to 0.5
- mod_gate: float32 [3072], replicated, may hold values from 0.5 to 1.5
- slot_tiles: int32 [16], replicated, may hold values from 0 to 15, as said below
- key_tiles: int32 [16, 27], replicated, may hold values from -1 to 15, as said below
Outputs:
- block_out: bfloat16 [6144, 3072], P('seq', 'hid')
Inputs may be any that keep to these rules, and one draw needn't show every extreme that they name: slot_tiles is a permutation of the tiles of a grid of 8 x 1 x 2, tile id (t + h) * 2 + w; two tiles that differ by at most one along every grid dimension sit at most 3 slots apart. `key_tiles`: row q lists distinct tile ids, each within one step of tile q along every grid dimension, in a fixed order of the 27 offsets; column 13 is q itself; other entries are -1.
All inputs are finite; a program needn't handle non-finite values.
Results may differ from a plain program's by a relative error of at most 0.0052.
Values may be sent and summed in bfloat16 or wider, within the bound.
A program may use at most 128 MiB of HBM per device.

v0:
```python
import math

import jax
import jax.numpy as jnp
from jax import lax
from jax.sharding import PartitionSpec as P

HEAD_DIM = 128
TILE = 384
REACH = 3


def passed_along(value, axis, steps):
    count = lax.axis_size(axis)
    initial, last = (max(0, -steps), min(count, count - steps))
    return lax.ppermute(value, axis, [(source, source + steps) for source in range(initial, last)])


def attend_rows(query_rows, key_rows, value_rows, allowed):
    head_count = query_rows.shape[1] // HEAD_DIM
    q_heads = jnp.transpose(
        query_rows.reshape(query_rows.shape[0], head_count, HEAD_DIM), (1, 0, 2)
    )
    k_heads = jnp.transpose(key_rows.reshape(key_rows.shape[0], head_count, HEAD_DIM), (1, 0, 2))
    v_heads = jnp.transpose(
        value_rows.reshape(value_rows.shape[0], head_count, HEAD_DIM), (1, 0, 2)
    )

    def one_head(operands):
        q_one, k_one, v_one = operands
        scores = lax.dot_general(
            q_one, k_one, (((1,), (1,)), ((), ())), preferred_element_type=jnp.float32
        )
        scores = scores * (1.0 / math.sqrt(HEAD_DIM))
        scores = jnp.where(allowed, scores, -jnp.inf)
        row_max = jnp.max(scores, axis=-1, keepdims=True)
        probs = jnp.exp(scores - row_max)
        row_total = jnp.sum(probs, axis=-1)
        blended = jnp.dot(probs.astype(jnp.bfloat16), v_one, preferred_element_type=jnp.float32)
        return (blended / row_total[:, None]).astype(jnp.bfloat16)

    mixed = lax.map(one_head, (q_heads, k_heads, v_heads))
    return jnp.transpose(mixed, (1, 0, 2)).reshape(query_rows.shape[0], -1)


def on_device(
    queries, keys, values, residual, w_in, w_out, mod_scale, mod_gate, slot_tiles, key_tiles
):
    tok_rows, width = queries.shape
    stacked = jnp.stack((keys, values))
    hop_count = -(-(REACH * TILE) // tok_rows)
    offsets = list(range(hop_count, 0, -1)) + [0] + list(range(-1, -hop_count - 1, -1))
    pieces = []
    for hop_dist in offsets:
        if hop_dist == 0:
            pieces.append(stacked)
        else:
            pieces.append(passed_along(stacked, "seq", hop_dist))
    window_rows = jnp.concatenate(pieces, axis=1)
    padded_keys = window_rows[0]
    padded_values = window_rows[1]
    tile_count = tok_rows // TILE
    span = tile_count + 2 * REACH
    tile_total = slot_tiles.shape[0]
    first_slot = lax.axis_index("seq") * tile_count
    buffer_slots = first_slot - REACH + jnp.arange(span, dtype=jnp.int32)
    inside = (buffer_slots >= 0) & (buffer_slots < tile_total)
    buffer_tiles = slot_tiles[jnp.clip(buffer_slots, 0, tile_total - 1)]
    own_tiles = lax.dynamic_slice_in_dim(slot_tiles, first_slot, tile_count)
    wanted = key_tiles[own_tiles]
    listed = jnp.any(wanted[:, :, None] == buffer_tiles[None, None, :], axis=1) & inside[None, :]
    distance = (
        jnp.arange(span, dtype=jnp.int32)[None, :]
        - jnp.arange(tile_count, dtype=jnp.int32)[:, None]
    )
    near_ok = (distance >= 0) & (distance <= 2 * REACH)
    tile_mask = listed & near_ok
    row_mask = jnp.repeat(jnp.repeat(tile_mask, TILE, axis=0), TILE, axis=1)
    attn = attend_rows(queries, padded_keys, padded_values, row_mask)
    combined = (residual.astype(jnp.float32) + attn.astype(jnp.float32)).astype(jnp.bfloat16)
    whole = lax.all_gather(combined, "hid", axis=1, tiled=True)
    wide = whole.astype(jnp.float32)
    square = jnp.mean(wide * wide, axis=-1, keepdims=True)
    normed = (wide * lax.rsqrt(square + 1e-06) * (1.0 + mod_scale)).astype(jnp.bfloat16)
    inner = jnp.dot(normed, w_in, preferred_element_type=jnp.float32)
    hidden = jax.nn.gelu(inner, approximate=True).astype(jnp.bfloat16)
    terms = jnp.dot(
        hidden, lax.all_gather(w_out, "seq", axis=1, tiled=True), preferred_element_type=jnp.float32
    )
    mlp_part = lax.psum_scatter(terms, "hid", scatter_dimension=1, tiled=True)
    gate_part = lax.dynamic_slice_in_dim(mod_gate, lax.axis_index("hid") * width, width)
    return (combined.astype(jnp.float32) + gate_part * mlp_part).astype(jnp.bfloat16)


def solution(mesh):
    placed = (
        P("seq", "hid"),
        P("seq", "hid"),
        P("seq", "hid"),
        P("seq", "hid"),
        P(None, "hid"),
        P("hid", "seq"),
        P(),
        P(),
        P(),
        P(),
    )
    return jax.shard_map(
        on_device, mesh=mesh, in_specs=placed, out_specs=P("seq", "hid"), check_vma=False
    )
```

profile of v0, /device:TPU:0, one launch (start us, length us, event | category | flops | bytes accessed | tf_op | source)
XLA Modules:
  0.0 531.4 jit_solution(9454319776741406526)
XLA Ops:
  6.5 1.7 copy.21
  8.3 1.7 copy.22
  11.7 5.7 %collective-permute-start = (bf16[2,384,1536]{1,2,0:T(8,128)(2,1)}, bf16[2,384,1536]{1,2,0:T(8,128)(2,1)}, u32[]{:S(2)}, u32[]{:S(2)}) collective-permute-start(bf16[2,384,1536]{1,2,0:T(8,128)(2,1)} %pad_maximum_fusion), channel_id=1, source_target_pairs={{0,6},{2,8},{4,10},{6,12},{8,14},{10,16},{12,18},{14,20},{16,22},{... | collective-permute-start | bytes 7077896 | tf_op jit(solution)/shard_map/ppermute | solution.py:16
  17.4 4.8 collective-permute-start.1
  22.2 2.8 collective-permute-start.2
  29.7 136.1 %collective-permute-done = bf16[2,384,1536]{1,2,0:T(8,128)(2,1)} collective-permute-done((bf16[2,384,1536]{1,2,0:T(8,128)(2,1)}, bf16[2,384,1536]{1,2,0:T(8,128)(2,1)}, u32[]{:S(2)}, u32[]{:S(2)}) %collective-permute-start) | collective-permute-done | bytes 2359328 | tf_op jit(solution)/shard_map/ppermute | solution.py:16
  168.7 1.7 copy.20
  170.4 1.9 constant_dynamic-update-slice_fusion.7
  172.3 44.0 %collective-permute-done.1 = bf16[2,384,1536]{1,2,0:T(8,128)(2,1)} collective-permute-done((bf16[2,384,1536]{1,2,0:T(8,128)(2,1)}, bf16[2,384,1536]{1,2,0:T(8,128)(2,1)}, u32[]{:S(2)}, u32[]{:S(2)}) %collective-permute-start.1) | collective-permute-done | bytes 2359328 | tf_op jit(solution)/shard_map/ppermute | solution.py:16
  216.3 2.1 constant_dynamic-update-slice_fusion.6
  218.5 2.1 constant_dynamic-update-slice_fusion.5
  221.1 2.1 constant_dynamic-update-slice_fusion.3
  223.2 2.1 constant_dynamic-update-slice_fusion.2
  225.4 2.1 constant_dynamic-update-slice_fusion.1
  227.6 6.0 %fusion.56 = (bf16[1,2688,1536]{1,2,0:T(8,128)(2,1)}, bf16[1,2688,1536]{1,2,0:T(8,128)(2,1)}) fusion(bf16[2,2688,1536]{1,2,0:T(8,128)(2,1)S(1)} %constant_dynamic-update-slice_fusion.1), kind=kLoop, calls=%fused_computation.66 | loop fusion | bytes 33030144 | tf_op jit(solution)/shard_map/slice | solution.py:61
  233.5 56.9 %while.12 = (s32[]{:T(128)}, bf16[12,384,128]{1,2,0:T(8,128)(2,1)S(1)}, bf16[12,384,128]{1,2,0:T(8,128)(2,1)S(1)}, bf16[12,2688,128]{1,2,0:T(8,128)(2,1)}, bf16[...) while((s32[]{:T(128)}, bf16[12,384,128]{1,2,0:T(8,128)(2,1)S(1)}, ...), condition=%wide.region_4.5_spmd.clone, body=%wide.region_1.4_spmd.clone.sunk | while | flops 535805184 | bytes 14364753 | solution.py:42
  233.5 2.0 fusion.66
  236.2 1.9 fusion.68
  238.3 2.0 fusion.66
  240.9 1.9 fusion.68
  243.0 2.0 fusion.66
  245.7 1.9 fusion.68
  247.7 2.0 fusion.66
  250.4 1.9 fusion.68
  252.5 2.0 fusion.66
  255.2 1.9 fusion.68
  257.2 2.0 fusion.66
  259.9 1.9 fusion.68
  262.0 2.0 fusion.66
  264.6 1.9 fusion.68
  266.7 2.0 fusion.66
  269.4 1.9 fusion.68
  271.4 2.0 fusion.66
  274.1 1.9 fusion.68
  276.2 2.0 fusion.66
  278.9 1.9 fusion.68
  280.9 2.0 fusion.66
  283.6 1.9 fusion.68
  285.7 2.0 fusion.66
  288.3 1.9 fusion.68
  290.6 2.1 copy.27
  292.7 3.1 add_convert_fusion.1
  296.8 37.5 %all-gather.3.cloned.1.call-done = bf16[384,3072]{1,0:T(8,128)(2,1)} async-done(((bf16[384,1536]{1,0:T(8,128)(2,1)}), bf16[384,3072]{1,0:T(8,128)(2,1)}) %all-gather.3.cloned.1.call-update) | async-done | bytes 2359312 | tf_op jit(solution)/shard_map/all_gather | solution.py:81
  334.3 2.2 fusion.25
  336.6 98.4 %all-gather.5.cloned.1.call-done = bf16[3072,3072]{0,1:T(8,128)(2,1)} async-done(((bf16[3072,192]{0,1:T(8,128)(2,1)}), bf16[3072,3072]{0,1:T(8,128)(2,1)}) %all-gather.5.cloned.1.call-update) | async-done | bytes 18874384 | tf_op jit(solution)/shard_map/all_gather | solution.py:88
  434.9 26.7 %fusion.36 = f32[384,3072]{1,0:T(8,128)} fusion(bf16[3072,3072]{0,1:T(8,128)(2,1)} %all-gather.5.cloned.1.call-done, bf16[3072,3072]{1,0:T(8,128)(2,1)} %param.16, bf16[384,3072]{1,0:T(8,128)(2,1)} %all-gather.3.cloned.1.call-done, f32[3072]{0:T(1024)S(1)} %broadcast_add_fusion, f32[384]{0:T(512)S(1)} %add_rsqrt_fusion), kind=kOutput, calls=%fused_computation.35 | convolution fusion | flops 14510850048 | bytes 44840448 | tf_op jit(solution)/shard_map/dot_general | solution.py:87
  462.5 59.4 %reduce-scatter.2.cloned.1.call-done = f32[384,1536]{1,0:T(8,128)} async-done(((f32[384,3072]{1,0:T(8,128)}), f32[384,1536]{1,0:T(8,128)}) %reduce-scatter.2.cloned.1.call-update) | async-done | bytes 2359312 | tf_op jit(solution)/shard_map/reduce_scatter | solution.py:90
  521.8 3.0 add_convert_fusion
  (81 shorter events, 19.8 us)
Async XLA Ops:
  6.5 161.9 %copy-start = (s32[16,27]{1,0:T(8,128)S(1)}, s32[16,27]{1,0:T(8,128)}, u32[]{:S(2)}) copy-start(s32[16,27]{1,0:T(8,128)} %param.21) | copy-start | bytes 5188
  6.5 327.8 %all-gather.3.cloned.1.call-start = ((), (), s32[]{:S(2)}) async-start(), calls=%async_computation.1 | async-start | bytes 3538944 | tf_op jit(solution)/shard_map/all_gather | solution.py:81
  8.3 19.3 %copy-start.2 = (s32[16]{0:T(128)S(1)}, s32[16]{0:T(128)}, u32[]{:S(2)}) copy-start(s32[16]{0:T(128)} %param.20) | copy-start | bytes 196
  11.7 154.1 %collective-permute-start = (bf16[2,384,1536]{1,2,0:T(8,128)(2,1)}, bf16[2,384,1536]{1,2,0:T(8,128)(2,1)}, u32[]{:S(2)}, u32[]{:S(2)}) collective-permute-start(bf16[2,384,1536]{1,2,0:T(8,128)(2,1)} %pad_maximum_fusion), channel_id=1, source_target_pairs={{0,6},{2,8},{4,10},{6,12},{8,14},{10,16},{12,18},{14,20},{16,22},{... | collective-permute-start | bytes 7077896 | tf_op jit(solution)/shard_map/ppermute | solution.py:16
  17.4 198.9 %collective-permute-start.1 = (bf16[2,384,1536]{1,2,0:T(8,128)(2,1)}, bf16[2,384,1536]{1,2,0:T(8,128)(2,1)}, u32[]{:S(2)}, u32[]{:S(2)}) collective-permute-start(bf16[2,384,1536]{1,2,0:T(8,128)(2,1)} %pad_maximum_fusion), channel_id=1, source_target_pairs={{0,4},{2,6},{4,8},{6,10},{8,12},{10,14},{12,16},{14,18},{16,20},{1... | collective-permute-start | bytes 7077896 | tf_op jit(solution)/shard_map/ppermute | solution.py:16
  22.2 196.2 %collective-permute-start.2 = (bf16[2,384,1536]{1,2,0:T(8,128)(2,1)}, bf16[2,384,1536]{1,2,0:T(8,128)(2,1)}, u32[]{:S(2)}, u32[]{:S(2)}) collective-permute-start(bf16[2,384,1536]{1,2,0:T(8,128)(2,1)} %pad_maximum_fusion), channel_id=1, source_target_pairs={{0,2},{2,4},{4,6},{6,8},{8,10},{10,12},{12,14},{14,16},{16,18},{18... | collective-permute-start | bytes 7077896 | tf_op jit(solution)/shard_map/ppermute | solution.py:16
  25.0 196.1 %collective-permute-start.3 = (bf16[2,384,1536]{1,2,0:T(8,128)(2,1)}, bf16[2,384,1536]{1,2,0:T(8,128)(2,1)}, u32[]{:S(2)}, u32[]{:S(2)}) collective-permute-start(bf16[2,384,1536]{1,2,0:T(8,128)(2,1)} %pad_maximum_fusion), channel_id=1, source_target_pairs={{2,0},{4,2},{6,4},{8,6},{10,8},{12,10},{14,12},{16,14},{18,16},{20... | collective-permute-start | bytes 7077896 | tf_op jit(solution)/shard_map/ppermute | solution.py:16
  26.3 197.0 %collective-permute-start.4 = (bf16[2,384,1536]{1,2,0:T(8,128)(2,1)}, bf16[2,384,1536]{1,2,0:T(8,128)(2,1)}, u32[]{:S(2)}, u32[]{:S(2)}) collective-permute-start(bf16[2,384,1536]{1,2,0:T(8,128)(2,1)} %pad_maximum_fusion), channel_id=1, source_target_pairs={{4,0},{6,2},{8,4},{10,6},{12,8},{14,10},{16,12},{18,14},{20,16},{2... | collective-permute-start | bytes 7077896 | tf_op jit(solution)/shard_map/ppermute | solution.py:16
  165.7 59.6 %collective-permute-start.5 = (bf16[2,384,1536]{1,2,0:T(8,128)(2,1)}, bf16[2,384,1536]{1,2,0:T(8,128)(2,1)}, u32[]{:S(2)}, u32[]{:S(2)}) collective-permute-start(bf16[2,384,1536]{1,2,0:T(8,128)(2,1)} %pad_maximum_fusion), channel_id=1, source_target_pairs={{6,0},{8,2},{10,4},{12,6},{14,8},{16,10},{18,12},{20,14},{22,16},{... | collective-permute-start | bytes 7077896 | tf_op jit(solution)/shard_map/ppermute | solution.py:16
  227.5 6.0 %copy-start.4 = (bf16[12,384,128]{1,2,0:T(8,128)(2,1)S(1)}, bf16[12,384,128]{1,2,0:T(8,128)(2,1)}, u32[]{:S(2)}) copy-start(bf16[12,384,128]{1,2,0:T(8,128)(2,1)} %custom-call.3) | copy-start | bytes 3538948
  290.6 2.1 copy-start.5
  292.7 4.1 copy-start.6
  295.8 139.1 %all-gather.5.cloned.1.call-start = ((), (), s32[]{:S(2)}) async-start(), calls=%async_computation.2 | async-start | bytes 20054016 | tf_op jit(solution)/shard_map/all_gather | solution.py:88
  296.6 225.3 %reduce-scatter.2.cloned.1.call-start = ((), (), s32[]{:S(2)}) async-start(), calls=%async_computation.3 | async-start | bytes 7077888 | tf_op jit(solution)/shard_map/reduce_scatter | solution.py:90
  461.7 0.7 copy-start.7
  461.7 60.2 %copy-start.3 = (bf16[384,1536]{1,0:T(8,128)(2,1)S(1)}, bf16[384,1536]{1,0:T(8,128)(2,1)}, u32[]{:S(2)}) copy-start(bf16[384,1536]{1,0:T(8,128)(2,1)} %add_convert_fusion.1) | copy-start | bytes 3538948
  461.7 63.2 %copy-start.1 = (s32[16,27]{1,0:T(8,128)S(1)}, s32[16,27]{1,0:T(8,128)}, u32[]{:S(2)}) copy-start(s32[16,27]{1,0:T(8,128)} %param.21) | copy-start | bytes 5188
Sparse Core Ops, SparseCore 0:
  295.9 38.3 all-gather.2
  335.9 98.9 all-gather.4
  461.8 59.9 reduce-scatter.1
where the time goes:
time: 533 us; the launch traced here: 531 us
  waiting for transfers between devices  376 us (71%)
  matrix products  73 us (14%)
  local copies, waits for them, and re-layouts  29.7 us (6%)
  other arithmetic  19.3 us (4%)
  starting transfers between devices  17.4 us (3%)
  between operations  15.4 us (3%)
    ppermute x6, waiting for transfers between devices, passed_along(): lax.ppermute(value, axis, [(source, source + steps) for source in range(i...  180 us
    all_gather x1, waiting for transfers between devices, on_device(): lax.all_gather(w_out, 'seq', axis=1, tiled=True)  98.4 us
    reduce_scatter x1, waiting for transfers between devices, on_device(): mlp_part = lax.psum_scatter(terms, 'hid', scatter_dimension=1, tiled=True)  59.4 us
    all_gather x1, waiting for transfers between devices, on_device(): whole = lax.all_gather(combined, 'hid', axis=1, tiled=True)  37.5 us
    dot_general x1, matrix products, on_device(): jnp.dot(hidden, lax.all_gather(w_out, 'seq', axis=1, tiled=True), preferr...  26.7 us
    dot_general x12, matrix products, one_head(): lax.dot_general(q_one, k_one, (((1,), (1,)), ((), ())), preferred_element...  23.6 us
    dot_general x12, matrix products, one_head(): jnp.dot(probs.astype(jnp.bfloat16), v_one, preferred_element_type=jnp.flo...  22.7 us
    ppermute x6, starting transfers between devices, passed_along(): lax.ppermute(value, axis, [(source, source + steps) for source in range(i...  17.2 us
  transfers between devices with their start and end apart: 9, of which 5 were waited for; matrix products, arithmetic and copies ran while one was open for 3% of the time, Pallas kernels for 0%

commit v1 on v0

v1 whole, which is shorter than its diff:
```python
import functools
import math

import jax
import jax.numpy as jnp
from jax import lax
from jax.experimental import pallas as pl
from jax.experimental.pallas import tpu as pltpu
from jax.sharding import PartitionSpec as P

HEAD_DIM = 128
TILE = 384
SLOTS = 6
GROUP = 256
W_CHUNK = 512
UNIT = 384
MESH = pl.DeviceIdType.MESH


def block_kernel(
    chips,
    q_ref, res_ref, bias_ref, scale_ref, gate_ref, k_hbm, v_hbm, win_hbm, wout_hbm,
    out_ref,
    kv, wout, win, comb, normed, hidden, term_out, term_in,
    local_sem, win_sem, near_s, near_r, far_s, far_r, own_s, own_r, cn_s, cn_r, cf_s, cf_r,
    x_s, x_r, ring_s, ring_r, cring_s, cring_r, wown_s, wown_r, term_s, term_r,
):
    seq = lax.axis_index("seq")
    hid = lax.axis_index("hid")
    chip, core = seq // 2, seq % 2
    odd = chip % 2
    rows, width = q_ref.shape
    depth = win_hbm.shape[0]
    units = win_hbm.shape[1]
    groups = width // GROUP
    w_rows = wout_hbm.shape[0]
    half_ring = chips // 2

    def at(chip_index, core_index):
        return {"seq": chip_index * 2 + core_index}

    mate = at(chip, 1 - core)
    near = at(chip + 1 - 2 * odd, core)
    step = 2 - 4 * odd
    has_far = (chip - step >= 0) & (chip - step < chips)
    has_fwd = (chip + step >= 0) & (chip + step < chips)
    ahead = at(chip + step, core)
    behind = at(chip - step, core)
    peer = {"hid": 1 - hid}

    place = jnp.where(odd == 0, chip // 2, chips - 1 - chip // 2)

    def ring_chip(position):
        position = (position + 2 * chips) % chips
        return jnp.where(position < half_ring, 2 * position, 2 * (chips - 1 - position) + 1)

    ring_next = at(ring_chip(place + 1), core)
    ring_prev = at(ring_chip(place - 1), core)

    near_row = (4 - 4 * odd) * TILE
    far_row = 4 * odd * TILE
    mid_row = 2 * TILE

    def kv_rows(base, which):
        return pl.ds(pl.multiple_of(base + which * TILE, TILE), TILE)

    def cols(g):
        return pl.ds(pl.multiple_of(g * GROUP, GROUP), GROUP)

    def remote(src, dst, send, recv, device):
        return pltpu.make_async_remote_copy(
            src_ref=src, dst_ref=dst, send_sem=send, recv_sem=recv,
            device_id=device, device_id_type=MESH,
        )

    def mine(g):
        return kv.at[:, kv_rows(mid_row, core), cols(g)]

    def near_copy(g):
        return remote(
            mine(g), kv.at[:, kv_rows(far_row, core), cols(g)], near_s.at[g], near_r.at[g], near
        )

    def far_copy(g):
        return remote(
            kv.at[:, kv_rows(near_row, core), cols(g)],
            kv.at[:, kv_rows(far_row, core), cols(g)], far_s.at[g], far_r.at[g], ahead,
        )

    def mate_copy(base, send, recv, g):
        part = kv.at[:, kv_rows(base, core), cols(g)]
        return remote(part, part, send.at[g], recv.at[g], mate)

    def own_copy(g):
        return mate_copy(mid_row, own_s, own_r, g)

    def cn_copy(g):
        return mate_copy(near_row, cn_s, cn_r, g)

    def cf_copy(g):
        return mate_copy(far_row, cf_s, cf_r, g)

    def comb_cols(g):
        return pl.ds(pl.multiple_of(hid * width + g * GROUP, GROUP), GROUP)

    def x_copy(g):
        part = comb.at[:, comb_cols(g)]
        return remote(part, part, x_s.at[g], x_r.at[g], peer)

    def wout_part(chip_index, core_index, lanes):
        row = pl.multiple_of((chip_index * 2 + core_index) * w_rows, w_rows)
        return wout.at[pl.ds(row, w_rows), lanes]

    def lanes_of(way, t):
        if t < half_ring:
            return pl.ds(0, units)
        return pl.ds(way * (units // 2), units // 2)

    def ring_copy(way, t):
        source = ring_chip(place - (t - 1) if way == 0 else place + (t - 1))
        part = wout_part(source, core, lanes_of(way, t))
        return remote(
            part, part, ring_s.at[way, t - 1], ring_r.at[way, t - 1],
            ring_next if way == 0 else ring_prev,
        )

    def ring_mate(way, t):
        source = ring_chip(place - t if way == 0 else place + t)
        part = wout_part(source, core, lanes_of(way, t))
        return remote(part, part, cring_s.at[way, t - 1], cring_r.at[way, t - 1], mate)

    def ring_step(t):
        for way in range(2):
            ring_copy(way, t).wait_recv()
            if t < half_ring:
                ring_copy(way, t + 1).start()
            ring_mate(way, t).start()

    def wown_copy():
        part = wout_part(chip, core, pl.ds(0, units))
        return remote(part, part, wown_s.at[0], wown_r.at[0], mate)

    def win_copy(j, slot):
        return pltpu.make_async_copy(
            win_hbm.at[:, pl.ds(pl.multiple_of(j * W_CHUNK, W_CHUNK), W_CHUNK)],
            win.at[slot], win_sem.at[slot],
        )

    def term_copy(j):
        return remote(term_out.at[j], term_in.at[j], term_s.at[j], term_r.at[j], peer)

    loads = [
        pltpu.make_async_copy(k_hbm, kv.at[0, kv_rows(mid_row, core), :], local_sem.at[0]),
        pltpu.make_async_copy(v_hbm, kv.at[1, kv_rows(mid_row, core), :], local_sem.at[1]),
        pltpu.make_async_copy(
            wout_hbm, wout_part(chip, core, pl.ds(0, units)), local_sem.at[2]
        ),
    ]
    for load in loads:
        load.start()
    win_copy(0, 0).start()
    win_copy(1, 1).start()

    barrier = pltpu.get_barrier_semaphore()
    for device in (mate, near, peer, ring_next, ring_prev):
        pl.semaphore_signal(barrier, inc=1, device_id=device, device_id_type=MESH)

    @pl.when(has_fwd)
    def _():
        pl.semaphore_signal(barrier, inc=1, device_id=ahead, device_id_type=MESH)

    @pl.when(has_far)
    def _():
        pl.semaphore_signal(barrier, inc=1, device_id=behind, device_id_type=MESH)

    pl.semaphore_wait(barrier, 5 + has_fwd.astype(jnp.int32) + has_far.astype(jnp.int32))

    loads[0].wait()
    loads[1].wait()

    def send_own(g, _):
        near_copy(g).start()
        own_copy(g).start()
        return 0

    lax.fori_loop(0, groups, send_own, 0)
    loads[2].wait()
    ring_copy(0, 1).start()
    ring_copy(1, 1).start()
    wown_copy().start()

    @pl.when(jnp.logical_not(has_far))
    def _():
        kv[:, pl.ds(pl.multiple_of(far_row, TILE), 2 * TILE), :] = jnp.zeros(
            (2, 2 * TILE, width), kv.dtype
        )

    def attend(g):
        def head(h, _):
            lanes = pl.ds(pl.multiple_of(g * GROUP + h * HEAD_DIM, HEAD_DIM), HEAD_DIM)
            scores = lax.dot_general(
                q_ref[:, lanes], kv[0, :, lanes], (((1,), (1,)), ((), ())),
                preferred_element_type=jnp.float32,
            )
            scores = scores * (1.0 / math.sqrt(HEAD_DIM)) + bias_ref[...]
            probs = jnp.exp(scores - jnp.max(scores, axis=-1, keepdims=True))
            total = jnp.sum(probs, axis=-1, keepdims=True)
            mixed = jnp.dot(
                probs.astype(jnp.bfloat16), kv[1, :, lanes], preferred_element_type=jnp.float32
            )
            attn = (mixed / total).astype(jnp.bfloat16)
            summed = res_ref[:, lanes].astype(jnp.float32) + attn.astype(jnp.float32)
            lanes_to = pl.ds(
                pl.multiple_of(hid * width + g * GROUP + h * HEAD_DIM, HEAD_DIM), HEAD_DIM
            )
            comb[:, lanes_to] = summed.astype(jnp.bfloat16)
            return 0

        lax.fori_loop(0, GROUP // HEAD_DIM, head, 0)

    def group_step(g, _):
        @pl.when(g < groups)
        def _():
            near_in = remote(
                mine(g), kv.at[:, kv_rows(near_row, core), cols(g)], near_s.at[g], near_r.at[g],
                near,
            )
            near_in.wait_recv()

            @pl.when(has_fwd)
            def _():
                far_copy(g).start()

            cn_copy(g).start()

        @pl.when(g >= 1)
        def _():
            prior = g - 1

            @pl.when(has_far)
            def _():
                far_copy(prior).wait_recv()
                cf_copy(prior).start()

            mate_in(own_r, mid_row, prior).wait_recv()
            mate_in(cn_r, near_row, prior).wait_recv()

            @pl.when(has_far)
            def _():
                mate_in(cf_r, far_row, prior).wait_recv()

            attend(prior)
            x_copy(prior).start()

        @pl.when(g == 3)
        def _():
            ring_step(1)

        return 0

    def mate_in(recv, base, g):
        part = kv.at[:, kv_rows(base, 1 - core), cols(g)]
        return remote(part, part, own_s.at[g], recv.at[g], mate)

    lax.fori_loop(0, groups + 1, group_step, 0)

    ring_step(2)

    def x_in(g, _):
        part = comb.at[:, pl.ds(pl.multiple_of((1 - hid) * width + g * GROUP, GROUP), GROUP)]
        remote(part, part, x_s.at[g], x_r.at[g], peer).wait_recv()
        return 0

    lax.fori_loop(0, groups, x_in, 0)

    norm_rows = 64

    def norm(i, _):
        block = pl.ds(pl.multiple_of(i * norm_rows, norm_rows), norm_rows)
        wide = comb[block, :].astype(jnp.float32)
        square = jnp.mean(wide * wide, axis=-1, keepdims=True)
        normed[block, :] = (
            wide * lax.rsqrt(square + 1e-06) * (1.0 + scale_ref[...])
        ).astype(jnp.bfloat16)
        return 0

    lax.fori_loop(0, rows // norm_rows, norm, 0)

    w_chunks = units // W_CHUNK

    def project(j, _):
        slot = j % 2
        win_copy(j, slot).wait()
        inner = jnp.dot(normed[...], win[slot], preferred_element_type=jnp.float32)
        hidden[:, pl.ds(pl.multiple_of(j * W_CHUNK, W_CHUNK), W_CHUNK)] = jax.nn.gelu(
            inner, approximate=True
        ).astype(jnp.bfloat16)

        @pl.when(j + 2 < w_chunks)
        def _():
            win_copy(j + 2, slot).start()

        return 0

    lax.fori_loop(0, w_chunks, project, 0)

    for t in range(3, half_ring + 1):
        ring_step(t)
    wown_in = wout_part(chip, 1 - core, pl.ds(0, units))
    remote(wown_in, wown_in, wown_s.at[0], wown_r.at[0], mate).wait_recv()
    for t in range(1, half_ring + 1):
        for way in range(2):
            source = ring_chip(place - t if way == 0 else place + t)
            part = wout_part(source, 1 - core, lanes_of(way, t))
            remote(part, part, cring_s.at[way, t - 1], cring_r.at[way, t - 1], mate).wait_recv()

    out_units = width // UNIT

    def terms(first, j):
        row = pl.multiple_of(first + j * UNIT, UNIT)
        return lax.dot_general(
            hidden[...], wout[pl.ds(row, UNIT), :], (((1,), (1,)), ((), ())),
            preferred_element_type=jnp.float32,
        )

    def away(j, _):
        term_out[j] = terms((1 - hid) * width, j).astype(jnp.bfloat16)
        term_copy(j).start()
        return 0

    lax.fori_loop(0, out_units, away, 0)

    def home(j, _):
        part = terms(hid * width, j)
        term_copy(j).wait_recv()
        lanes = pl.ds(pl.multiple_of(hid * width + j * UNIT, UNIT), UNIT)
        mlp = part + term_in[j].astype(jnp.float32)
        out_ref[:, pl.ds(pl.multiple_of(j * UNIT, UNIT), UNIT)] = (
            comb[:, lanes].astype(jnp.float32) + gate_ref[:, lanes] * mlp
        ).astype(jnp.bfloat16)
        return 0

    lax.fori_loop(0, out_units, home, 0)

    def sent(g, _):
        near_copy(g).wait_send()
        own_copy(g).wait_send()
        cn_copy(g).wait_send()
        x_copy(g).wait_send()

        @pl.when(has_fwd)
        def _():
            far_copy(g).wait_send()

        @pl.when(has_far)
        def _():
            cf_copy(g).wait_send()

        return 0

    lax.fori_loop(0, groups, sent, 0)
    for t in range(1, half_ring + 1):
        for way in range(2):
            ring_copy(way, t).wait_send()
            ring_mate(way, t).wait_send()
    wown_copy().wait_send()

    def term_sent(j, _):
        term_copy(j).wait_send()
        return 0

    lax.fori_loop(0, out_units, term_sent, 0)


def on_device(
    chips, queries, keys, values, residual, w_in, w_out, mod_scale, mod_gate, slot_tiles, key_tiles
):
    rows, width = queries.shape
    depth, units = w_in.shape
    groups = width // GROUP
    out_units = width // UNIT
    tile_total = slot_tiles.shape[0]
    slot = lax.axis_index("seq")
    near = (slot // 2) * 2 - 2 + jnp.arange(SLOTS, dtype=jnp.int32)
    inside = (near >= 0) & (near < tile_total)
    near_tiles = slot_tiles[jnp.clip(near, 0, tile_total - 1)]
    wanted = key_tiles[slot_tiles[slot]]
    listed = jnp.any(wanted[:, None] == near_tiles[None, :], axis=0) & inside
    bias = jnp.repeat(jnp.where(listed, 0.0, -jnp.inf).astype(jnp.float32), TILE)[None, :]

    vmem = pl.BlockSpec(memory_space=pltpu.VMEM)
    hbm = pl.BlockSpec(memory_space=pl.ANY)
    dma = pltpu.SemaphoreType.DMA
    half_ring = chips // 2
    return pl.pallas_call(
        functools.partial(block_kernel, chips),
        out_shape=jax.ShapeDtypeStruct((rows, width), jnp.bfloat16),
        in_specs=[vmem] * 5 + [hbm] * 4,
        out_specs=vmem,
        scratch_shapes=[
            pltpu.VMEM((2, SLOTS * TILE, width), jnp.bfloat16),
            pltpu.VMEM((depth, units), jnp.bfloat16),
            pltpu.VMEM((2, depth, W_CHUNK), jnp.bfloat16),
            pltpu.VMEM((rows, depth), jnp.bfloat16),
            pltpu.VMEM((rows, depth), jnp.bfloat16),
            pltpu.VMEM((rows, units), jnp.bfloat16),
            pltpu.VMEM((out_units, rows, UNIT), jnp.bfloat16),
            pltpu.VMEM((out_units, rows, UNIT), jnp.bfloat16),
            dma((3,)), dma((2,)),
        ] + [dma((groups,))] * 12 + [dma((2, half_ring))] * 4 + [dma((1,))] * 2
        + [dma((out_units,))] * 2,
        compiler_params=pltpu.CompilerParams(
            collective_id=0, has_side_effects=True, vmem_limit_bytes=62 * 1024 * 1024
        ),
    )(
        queries, residual, bias, mod_scale[None, :], mod_gate[None, :], keys, values, w_in,
        w_out.T,
    )


def solution(mesh):
    placed = (
        P("seq", "hid"),
        P("seq", "hid"),
        P("seq", "hid"),
        P("seq", "hid"),
        P(None, "hid"),
        P("hid", "seq"),
        P(),
        P(),
        P(),
        P(),
    )
    return jax.shard_map(
        functools.partial(on_device, mesh.shape["seq"] // 2),
        mesh=mesh, in_specs=placed, out_specs=P("seq", "hid"), check_vma=False,
    )
```

time: 533 us -> 219 us (0.41)
  waiting for transfers between devices: 376 us -> 0 us
  Pallas kernels: 0 us -> 209 us
  matrix products: 73 us -> 0 us
  local copies, waits for them, and re-layouts: 29.7 us -> 5.61 us
  other arithmetic: 19.3 us -> 0.21 us
  starting transfers between devices: 17.4 us -> 0 us
  between operations: 15.4 us -> 1.99 us
    pallas_call x0 -> x1, Pallas kernels: none -> 209 us  [on_device(): pl.pallas_call(functools.partial(block_kernel, chips), out_shape=jax.Shap...]
    ppermute x6 -> x0, waiting for transfers between devices: 180 us -> none  [passed_along(): lax.ppermute(value, axis, [(source, source + steps) for source in range(i...]
    all_gather x2 -> x0, waiting for transfers between devices: 136 us -> none  [the longest x1 98.4 us: on_device(): lax.all_gather(w_out, 'seq', axis=1, tiled=True)]
    dot_general x25 -> x0, matrix products: 73 us -> none  [the longest x1 26.7 us: on_device(): jnp.dot(hidden, lax.all_gather(w_out, 'seq', axis=1, tiled=True), preferr...]
    reduce_scatter x1 -> x0, waiting for transfers between devices: 59.4 us -> none  [on_device(): mlp_part = lax.psum_scatter(terms, 'hid', scatter_dimension=1, tiled=True)]
    ppermute x6 -> x0, starting transfers between devices: 17.2 us -> none  [passed_along(): lax.ppermute(value, axis, [(source, source + steps) for source in range(i...]
    unnamed x24 -> x5, local copies, waits for them, and re-layouts: 16.3 us -> 3.05 us
    reduce_sum x13 -> x0, other arithmetic: 10.6 us -> none  [the longest x12 8.44 us: one_head(): row_total = jnp.sum(probs, axis=-1)]
  transfers between devices with their start and end apart: 9 -> 0, of which waited for: 5 -> 0; matrix products, arithmetic and copies ran while one was open for 3% -> 0% of each run, Pallas kernels for 0% -> 0%
where the time goes in v1:
time: 219 us; the launch traced here: 217 us
  Pallas kernels  209 us (95%)
  local copies, waits for them, and re-layouts  5.61 us (3%)
    pallas_call x1, Pallas kernels, on_device(): pl.pallas_call(functools.partial(block_kernel, chips), out_shape=jax.Shap...  209 us

profile of v1, /device:TPU:0, one launch (start us, length us, event | category | flops | bytes accessed | tf_op | source)
XLA Modules:
  0.0 217.2 jit_solution(5299529312760477711)
XLA Ops:
  0.0 0.0 copy-start
  0.0 1.2 dynamic_slice.6
  3.2 0.0 copy-done
  3.3 1.3 gather_fusion
  4.6 0.2 compare_reduce_fusion
  4.8 0.1 broadcast_bitcast_fusion
  4.8 0.6 copy.11
  5.4 209.4 %shard_map.100 = bf16[384,1536]{1,0:T(8,128)(2,1)} custom-call(bf16[384,1536]{1,0:T(8,128)(2,1)} %q_ref.1, bf16[384,1536]{1,0:T(8,128)(2,1)} %res_ref.1, f32[1,2304]{1,0:T(1,128)} %bitcast.13, f32[1,3072]{1,0:T(1,128)} %bitcast.14, f32[1,3072]{1,0:T(1,128)} %bitcast.15, bf16[384,1536]{1,0:T(8,128)(2,1)} %k_hbm.1, bf16[384,1536]{1,0:T(8,128)(2,1)} %v_hbm.1, ...), custom_call_target="tpu_custom_call" | custom-call | tf_op jit(solution)/shard_map/pallas_call | solution.py:395
  214.8 2.4 %copy.13 = bf16[384,1536]{1,0:T(8,128)(2,1)} copy(bf16[384,1536]{1,0:T(8,128)(2,1)} %shard_map.100) | data formatting | bytes 2359296
  (4 shorter events, 0.0 us)
Async XLA Ops:
  0.0 3.2 %copy-start = (s32[16,27]{1,0:T(8,128)S(1)}, s32[16,27]{1,0:T(8,128)}, u32[]{:S(2)}) copy-start(s32[16,27]{1,0:T(8,128)} %param.19) | copy-start | bytes 5188

commit v2 on v1

--- a/solution.py
+++ b/solution.py
@@ -14,14 +14,16 @@
 GROUP = 256
 W_CHUNK = 512
 UNIT = 384
+RING_GROUPS = (1, 2, 4, 5)
+RING_CHUNK = 2
 MESH = pl.DeviceIdType.MESH
 
 
 def block_kernel(
     chips,
-    q_ref, res_ref, bias_ref, scale_ref, gate_ref, k_hbm, v_hbm, win_hbm, wout_hbm,
+    q_ref, res_ref, scale_ref, gate_ref, slot_ref, list_ref, k_hbm, v_hbm, win_hbm, wout_hbm,
     out_ref,
-    kv, wout, win, comb, normed, hidden, term_out, term_in,
+    kv, wout, win, comb, normed, hidden, term_out, term_in, term_home, bias_ref,
     local_sem, win_sem, near_s, near_r, far_s, far_r, own_s, own_r, cn_s, cn_r, cf_s, cf_r,
     x_s, x_r, ring_s, ring_r, cring_s, cring_r, wown_s, wown_r, term_s, term_r,
 ):
@@ -35,6 +37,8 @@
     groups = width // GROUP
     w_rows = wout_hbm.shape[0]
     half_ring = chips // 2
+    last = 2 * (half_ring - 1)
+    by_arrival = 2 * w_rows == UNIT
 
     def at(chip_index, core_index):
         return {"seq": chip_index * 2 + core_index}
@@ -111,30 +115,30 @@
         row = pl.multiple_of((chip_index * 2 + core_index) * w_rows, w_rows)
         return wout.at[pl.ds(row, w_rows), lanes]
 
-    def lanes_of(way, t):
-        if t < half_ring:
-            return pl.ds(0, units)
-        return pl.ds(way * (units // 2), units // 2)
-
-    def ring_copy(way, t):
-        source = ring_chip(place - (t - 1) if way == 0 else place + (t - 1))
-        part = wout_part(source, core, lanes_of(way, t))
+    def ring_part(way, s, away, core_index):
+        half = way if s == last else s % 2
+        source = ring_chip(place - away if way == 0 else place + away)
+        return wout_part(source, core_index, pl.ds(half * (units // 2), units // 2))
+
+    def ring_copy(way, s):
+        part = ring_part(way, s, s // 2, core)
         return remote(
-            part, part, ring_s.at[way, t - 1], ring_r.at[way, t - 1],
+            part, part, ring_s.at[way, s], ring_r.at[way, s],
             ring_next if way == 0 else ring_prev,
         )
 
-    def ring_mate(way, t):
-        source = ring_chip(place - t if way == 0 else place + t)
-        part = wout_part(source, core, lanes_of(way, t))
-        return remote(part, part, cring_s.at[way, t - 1], cring_r.at[way, t - 1], mate)
-
-    def ring_step(t):
+    def ring_mate(way, s, core_index):
+        part = ring_part(way, s, s // 2 + 1, core_index)
+        return remote(part, part, cring_s.at[way, s], cring_r.at[way, s], mate)
+
+    def ring_step(s):
         for way in range(2):
-            ring_copy(way, t).wait_recv()
-            if t < half_ring:
-                ring_copy(way, t + 1).start()
-            ring_mate(way, t).start()
+            ring_copy(way, s).wait_recv()
+            if s + 2 < last:
+                ring_copy(way, s + 2).start()
+            elif s < last and s % 2 == way:
+                ring_copy(way, last).start()
+            ring_mate(way, s, core).start()
 
     def wown_copy():
         part = wout_part(chip, core, pl.ds(0, units))
@@ -185,9 +189,23 @@
 
     lax.fori_loop(0, groups, send_own, 0)
     loads[2].wait()
-    ring_copy(0, 1).start()
-    ring_copy(1, 1).start()
+    for s in range(2):
+        ring_copy(0, s).start()
+        ring_copy(1, s).start()
     wown_copy().start()
+
+    tiles = slot_ref.shape[0]
+    own_tile = slot_ref[seq]
+    for i in range(SLOTS):
+        slot = 2 * chip - 2 + i
+        inside = ((slot >= 0) & (slot < tiles)).astype(jnp.int32)
+        tile = slot_ref[jnp.clip(slot, 0, tiles - 1)]
+        hits = jnp.int32(0)
+        for j in range(list_ref.shape[1]):
+            hits = hits + (list_ref[own_tile, j] == tile).astype(jnp.int32)
+        bias_ref[:, i * TILE : (i + 1) * TILE] = jnp.where(
+            jnp.full((1, TILE), hits * inside) > 0, 0.0, -jnp.inf
+        ).astype(jnp.float32)
 
     @pl.when(jnp.logical_not(has_far))
     def _():
@@ -252,9 +270,10 @@
             attend(prior)
             x_copy(prior).start()
 
-        @pl.when(g == 3)
-        def _():
-            ring_step(1)
+        for s, when in enumerate(RING_GROUPS):
+            @pl.when(g == when)
+            def _(s=s):
+                ring_step(s)
 
         return 0
 
@@ -263,8 +282,6 @@
         return remote(part, part, own_s.at[g], recv.at[g], mate)
 
     lax.fori_loop(0, groups + 1, group_step, 0)
-
-    ring_step(2)
 
     def x_in(g, _):
         part = comb.at[:, pl.ds(pl.multiple_of((1 - hid) * width + g * GROUP, GROUP), GROUP)]
@@ -300,19 +317,24 @@
         def _():
             win_copy(j + 2, slot).start()
 
+        @pl.when(j == RING_CHUNK)
+        def _():
+            ring_step(len(RING_GROUPS))
+
         return 0
 
     lax.fori_loop(0, w_chunks, project, 0)
 
-    for t in range(3, half_ring + 1):
-        ring_step(t)
+    handled = len(RING_GROUPS) + 1
     wown_in = wout_part(chip, 1 - core, pl.ds(0, units))
-    remote(wown_in, wown_in, wown_s.at[0], wown_r.at[0], mate).wait_recv()
-    for t in range(1, half_ring + 1):
-        for way in range(2):
-            source = ring_chip(place - t if way == 0 else place + t)
-            part = wout_part(source, 1 - core, lanes_of(way, t))
-            remote(part, part, cring_s.at[way, t - 1], cring_r.at[way, t - 1], mate).wait_recv()
+
+    def arrived(t):
+        if t == 0:
+            remote(wown_in, wown_in, wown_s.at[0], wown_r.at[0], mate).wait_recv()
+            return
+        for s in range(2 * t - 2, min(2 * t, last + 1)):
+            for way in range(2):
+                ring_mate(way, s, 1 - core).wait_recv()
 
     out_units = width // UNIT
 
@@ -323,24 +345,71 @@
             preferred_element_type=jnp.float32,
         )
 
-    def away(j, _):
+    def send_terms(j):
         term_out[j] = terms((1 - hid) * width, j).astype(jnp.bfloat16)
         term_copy(j).start()
-        return 0
-
-    lax.fori_loop(0, out_units, away, 0)
-
-    def home(j, _):
-        part = terms(hid * width, j)
+
+    def finish(j):
         term_copy(j).wait_recv()
         lanes = pl.ds(pl.multiple_of(hid * width + j * UNIT, UNIT), UNIT)
-        mlp = part + term_in[j].astype(jnp.float32)
+        mlp = term_home[j] + term_in[j].astype(jnp.float32)
         out_ref[:, pl.ds(pl.multiple_of(j * UNIT, UNIT), UNIT)] = (
             comb[:, lanes].astype(jnp.float32) + gate_ref[:, lanes] * mlp
         ).astype(jnp.bfloat16)
-        return 0
-
-    lax.fori_loop(0, out_units, home, 0)
+
+    def blocks_at(t):
+        if t == 0:
+            return [chip]
+        if t == half_ring:
+            return [ring_chip(place + t)]
+        return [ring_chip(place - t), ring_chip(place + t)]
+
+    if by_arrival:
+        for t in range(half_ring + 1):
+            if t > 0:
+                while handled < min(2 * t, last + 1):
+                    ring_step(handled)
+                    handled += 1
+            arrived(t)
+            for block in blocks_at(t):
+                home = block // out_units == hid
+                j = block % out_units
+
+                @pl.when(jnp.logical_not(home))
+                def _():
+                    send_terms(j)
+
+                @pl.when(home)
+                def _():
+                    term_home[j] = terms(hid * width, j)
+
+            for block in blocks_at(t - 1) if t > 0 else []:
+                @pl.when(block // out_units == hid)
+                def _():
+                    finish(block % out_units)
+
+        for block in blocks_at(half_ring):
+            @pl.when(block // out_units == hid)
+            def _():
+                finish(block % out_units)
+    else:
+        for s in range(handled, last + 1):
+            ring_step(s)
+        for t in range(half_ring + 1):
+            arrived(t)
+
+        def away(j, _):
+            send_terms(j)
+            return 0
+
+        lax.fori_loop(0, out_units, away, 0)
+
+        def at_home(j, _):
+            term_home[j] = terms(hid * width, j)
+            finish(j)
+            return 0
+
+        lax.fori_loop(0, out_units, at_home, 0)
 
     def sent(g, _):
         near_copy(g).wait_send()
@@ -359,10 +428,10 @@
         return 0
 
     lax.fori_loop(0, groups, sent, 0)
-    for t in range(1, half_ring + 1):
+    for s in range(last + 1):
         for way in range(2):
-            ring_copy(way, t).wait_send()
-            ring_mate(way, t).wait_send()
+            ring_copy(way, s).wait_send()
+            ring_mate(way, s, core).wait_send()
     wown_copy().wait_send()
 
     def term_sent(j, _):
@@ -379,23 +448,15 @@
     depth, units = w_in.shape
     groups = width // GROUP
     out_units = width // UNIT
-    tile_total = slot_tiles.shape[0]
-    slot = lax.axis_index("seq")
-    near = (slot // 2) * 2 - 2 + jnp.arange(SLOTS, dtype=jnp.int32)
-    inside = (near >= 0) & (near < tile_total)
-    near_tiles = slot_tiles[jnp.clip(near, 0, tile_total - 1)]
-    wanted = key_tiles[slot_tiles[slot]]
-    listed = jnp.any(wanted[:, None] == near_tiles[None, :], axis=0) & inside
-    bias = jnp.repeat(jnp.where(listed, 0.0, -jnp.inf).astype(jnp.float32), TILE)[None, :]
-
     vmem = pl.BlockSpec(memory_space=pltpu.VMEM)
+    smem = pl.BlockSpec(memory_space=pltpu.SMEM)
     hbm = pl.BlockSpec(memory_space=pl.ANY)
     dma = pltpu.SemaphoreType.DMA
     half_ring = chips // 2
     return pl.pallas_call(
         functools.partial(block_kernel, chips),
         out_shape=jax.ShapeDtypeStruct((rows, width), jnp.bfloat16),
-        in_specs=[vmem] * 5 + [hbm] * 4,
+        in_specs=[vmem] * 4 + [smem] * 2 + [hbm] * 4,
         out_specs=vmem,
         scratch_shapes=[
             pltpu.VMEM((2, SLOTS * TILE, width), jnp.bfloat16),
@@ -406,15 +467,17 @@
             pltpu.VMEM((rows, units), jnp.bfloat16),
             pltpu.VMEM((out_units, rows, UNIT), jnp.bfloat16),
             pltpu.VMEM((out_units, rows, UNIT), jnp.bfloat16),
+            pltpu.VMEM((out_units, rows, UNIT), jnp.float32),
+            pltpu.VMEM((1, SLOTS * TILE), jnp.float32),
             dma((3,)), dma((2,)),
-        ] + [dma((groups,))] * 12 + [dma((2, half_ring))] * 4 + [dma((1,))] * 2
+        ] + [dma((groups,))] * 12 + [dma((2, 2 * half_ring - 1))] * 4 + [dma((1,))] * 2
         + [dma((out_units,))] * 2,
         compiler_params=pltpu.CompilerParams(
             collective_id=0, has_side_effects=True, vmem_limit_bytes=62 * 1024 * 1024
         ),
     )(
-        queries, residual, bias, mod_scale[None, :], mod_gate[None, :], keys, values, w_in,
-        w_out.T,
+        queries, residual, mod_scale[None, :], mod_gate[None, :], slot_tiles, key_tiles,
+        keys, values, w_in, w_out.T,
     )
 
 

time: 219 us -> 215 us (0.982)
  local copies, waits for them, and re-layouts: 5.61 us -> 2.36 us
  Pallas kernels: 209 us -> 212 us
    pallas_call x1, Pallas kernels: 209 us -> 212 us  [on_device(): pl.pallas_call(functools.partial(block_kernel, chips), out_shape=jax.Shap...]
where the time goes in v2:
time: 215 us
  Pallas kernels  212 us (99%)
  local copies, waits for them, and re-layouts  2.36 us (1%)
    pallas_call x1, Pallas kernels, on_device(): pl.pallas_call(functools.partial(block_kernel, chips), out_shape=jax.Shap...  212 us

profile of v2, /device:TPU:0, one launch (start us, length us, event | category | flops | bytes accessed | tf_op | source)
XLA Modules:
  0.0 214.6 jit_solution(9685419649241070609)
XLA Ops:
  0.0 212.2 %shard_map.100 = bf16[384,1536]{1,0:T(8,128)(2,1)} custom-call(bf16[384,1536]{1,0:T(8,128)(2,1)} %q_ref.1, bf16[384,1536]{1,0:T(8,128)(2,1)} %res_ref.1, f32[1,3072]{1,0:T(1,128)} %bitcast.4, f32[1,3072]{1,0:T(1,128)} %bitcast.5, s32[16]{0:T(128)} %slot_ref.1, s32[16,27]{1,0:T(8,128)} %list_ref.1, bf16[384,1536]{1,0:T(8,128)(2,1)} %k_hbm.1, ...), custom_call_target="tpu_custom_call" | custom-call | tf_op jit(solution)/shard_map/pallas_call | solution.py:456
  212.3 2.4 %copy.12 = bf16[384,1536]{1,0:T(8,128)(2,1)} copy(bf16[384,1536]{1,0:T(8,128)(2,1)} %shard_map.100) | data formatting | bytes 2359296

commit v3 on v2

--- a/solution.py
+++ b/solution.py
@@ -14,8 +14,8 @@
 GROUP = 256
 W_CHUNK = 512
 UNIT = 384
-RING_GROUPS = (1, 2, 4, 5)
-RING_CHUNK = 2
+PASS_GROUPS = (3, 5)
+PASS_CHUNK = 2
 MESH = pl.DeviceIdType.MESH
 
 
@@ -25,7 +25,8 @@
     out_ref,
     kv, wout, win, comb, normed, hidden, term_out, term_in, term_home, bias_ref,
     local_sem, win_sem, near_s, near_r, far_s, far_r, own_s, own_r, cn_s, cn_r, cf_s, cf_r,
-    x_s, x_r, ring_s, ring_r, cring_s, cring_r, wown_s, wown_r, term_s, term_r,
+    x_s, x_r, up_s, up_r, over_s, over_r, cup_s, cup_r, cover_s, cover_r, wown_s, wown_r,
+    term_s, term_r,
 ):
     seq = lax.axis_index("seq")
     hid = lax.axis_index("hid")
@@ -36,8 +37,7 @@
     units = win_hbm.shape[1]
     groups = width // GROUP
     w_rows = wout_hbm.shape[0]
-    half_ring = chips // 2
-    last = 2 * (half_ring - 1)
+    column = chips // 2
     by_arrival = 2 * w_rows == UNIT
 
     def at(chip_index, core_index):
@@ -52,14 +52,16 @@
     behind = at(chip - step, core)
     peer = {"hid": 1 - hid}
 
-    place = jnp.where(odd == 0, chip // 2, chips - 1 - chip // 2)
-
-    def ring_chip(position):
-        position = (position + 2 * chips) % chips
-        return jnp.where(position < half_ring, 2 * position, 2 * (chips - 1 - position) + 1)
-
-    ring_next = at(ring_chip(place + 1), core)
-    ring_prev = at(ring_chip(place - 1), core)
+    place = chip // 2
+
+    def member(i, parity):
+        other = place
+        bit = 1
+        while bit <= i:
+            if i & bit:
+                other = other + bit - 2 * bit * ((place // bit) % 2)
+            bit *= 2
+        return 2 * other + parity
 
     near_row = (4 - 4 * odd) * TILE
     far_row = 4 * odd * TILE
@@ -115,30 +117,40 @@
         row = pl.multiple_of((chip_index * 2 + core_index) * w_rows, w_rows)
         return wout.at[pl.ds(row, w_rows), lanes]
 
-    def ring_part(way, s, away, core_index):
-        half = way if s == last else s % 2
-        source = ring_chip(place - away if way == 0 else place + away)
-        return wout_part(source, core_index, pl.ds(half * (units // 2), units // 2))
-
-    def ring_copy(way, s):
-        part = ring_part(way, s, s // 2, core)
-        return remote(
-            part, part, ring_s.at[way, s], ring_r.at[way, s],
-            ring_next if way == 0 else ring_prev,
-        )
-
-    def ring_mate(way, s, core_index):
-        part = ring_part(way, s, s // 2 + 1, core_index)
-        return remote(part, part, cring_s.at[way, s], cring_r.at[way, s], mate)
-
-    def ring_step(s):
-        for way in range(2):
-            ring_copy(way, s).wait_recv()
-            if s + 2 < last:
-                ring_copy(way, s + 2).start()
-            elif s < last and s % 2 == way:
-                ring_copy(way, last).start()
-            ring_mate(way, s, core).start()
+    every = pl.ds(0, units)
+
+    def up_copy(i):
+        part = wout_part(chip, core, every)
+        return remote(part, part, up_s.at[i], up_r.at[i], at(member(i, odd), core))
+
+    def up_in(i):
+        part = wout_part(member(i, odd), core, every)
+        return remote(part, part, up_s.at[i], up_r.at[i], at(member(i, odd), core))
+
+    def over_copy(i):
+        part = wout_part(member(i, odd), core, every)
+        return remote(part, part, over_s.at[i], over_r.at[i], near)
+
+    def over_in(i):
+        part = wout_part(member(i, 1 - odd), core, every)
+        return remote(part, part, over_s.at[i], over_r.at[i], near)
+
+    def up_mate(i, core_index):
+        part = wout_part(member(i, odd), core_index, every)
+        return remote(part, part, cup_s.at[i], cup_r.at[i], mate)
+
+    def over_mate(i, core_index):
+        part = wout_part(member(i, 1 - odd), core_index, every)
+        return remote(part, part, cover_s.at[i], cover_r.at[i], mate)
+
+    def pass_up(i):
+        up_in(i).wait_recv()
+        over_copy(i).start()
+        up_mate(i, core).start()
+
+    def pass_over(i):
+        over_in(i).wait_recv()
+        over_mate(i, core).start()
 
     def wown_copy():
         part = wout_part(chip, core, pl.ds(0, units))
@@ -166,7 +178,8 @@
     win_copy(1, 1).start()
 
     barrier = pltpu.get_barrier_semaphore()
-    for device in (mate, near, peer, ring_next, ring_prev):
+    members = [at(member(i, odd), core) for i in range(1, column)]
+    for device in [mate, near, peer] + members:
         pl.semaphore_signal(barrier, inc=1, device_id=device, device_id_type=MESH)
 
     @pl.when(has_fwd)
@@ -177,7 +190,7 @@
     def _():
         pl.semaphore_signal(barrier, inc=1, device_id=behind, device_id_type=MESH)
 
-    pl.semaphore_wait(barrier, 5 + has_fwd.astype(jnp.int32) + has_far.astype(jnp.int32))
+    pl.semaphore_wait(barrier, column + 2 + has_fwd.astype(jnp.int32) + has_far.astype(jnp.int32))
 
     loads[0].wait()
     loads[1].wait()
@@ -187,11 +200,14 @@
         own_copy(g).start()
         return 0
 
-    lax.fori_loop(0, groups, send_own, 0)
+    lax.fori_loop(0, 2, send_own, 0)
     loads[2].wait()
-    for s in range(2):
-        ring_copy(0, s).start()
-        ring_copy(1, s).start()
+    up_copy(1).start()
+    lax.fori_loop(2, 4, send_own, 0)
+    for i in range(2, column):
+        up_copy(i).start()
+    lax.fori_loop(4, groups, send_own, 0)
+    over_copy(0).start()
     wown_copy().start()
 
     tiles = slot_ref.shape[0]
@@ -270,10 +286,10 @@
             attend(prior)
             x_copy(prior).start()
 
-        for s, when in enumerate(RING_GROUPS):
+        for i, when in enumerate(PASS_GROUPS):
             @pl.when(g == when)
-            def _(s=s):
-                ring_step(s)
+            def _():
+                pass_up(i + 1)
 
         return 0
 
@@ -282,6 +298,9 @@
         return remote(part, part, own_s.at[g], recv.at[g], mate)
 
     lax.fori_loop(0, groups + 1, group_step, 0)
+    for i in range(len(PASS_GROUPS) + 1, column):
+        pass_up(i)
+    pass_over(0)
 
     def x_in(g, _):
         part = comb.at[:, pl.ds(pl.multiple_of((1 - hid) * width + g * GROUP, GROUP), GROUP)]
@@ -317,24 +336,30 @@
         def _():
             win_copy(j + 2, slot).start()
 
-        @pl.when(j == RING_CHUNK)
-        def _():
-            ring_step(len(RING_GROUPS))
+        @pl.when(j == PASS_CHUNK)
+        def _():
+            pass_over(1)
 
         return 0
 
     lax.fori_loop(0, w_chunks, project, 0)
 
-    handled = len(RING_GROUPS) + 1
-    wown_in = wout_part(chip, 1 - core, pl.ds(0, units))
-
-    def arrived(t):
-        if t == 0:
-            remote(wown_in, wown_in, wown_s.at[0], wown_r.at[0], mate).wait_recv()
-            return
-        for s in range(2 * t - 2, min(2 * t, last + 1)):
-            for way in range(2):
-                ring_mate(way, s, 1 - core).wait_recv()
+    wown_in = wout_part(chip, 1 - core, every)
+
+    def own_arrived():
+        remote(wown_in, wown_in, wown_s.at[0], wown_r.at[0], mate).wait_recv()
+
+    def up_arrived(i):
+        up_mate(i, 1 - core).wait_recv()
+
+    def over_arrived(i):
+        if i >= 2:
+            pass_over(i)
+        over_mate(i, 1 - core).wait_recv()
+
+    order = [(own_arrived, chip)]
+    order += [(functools.partial(up_arrived, i), member(i, odd)) for i in range(1, column)]
+    order += [(functools.partial(over_arrived, i), member(i, 1 - odd)) for i in range(column)]
 
     out_units = width // UNIT
 
@@ -357,46 +382,29 @@
             comb[:, lanes].astype(jnp.float32) + gate_ref[:, lanes] * mlp
         ).astype(jnp.bfloat16)
 
-    def blocks_at(t):
-        if t == 0:
-            return [chip]
-        if t == half_ring:
-            return [ring_chip(place + t)]
-        return [ring_chip(place - t), ring_chip(place + t)]
+    def finish_block(block):
+        @pl.when(block // out_units == hid)
+        def _():
+            finish(block % out_units)
 
     if by_arrival:
-        for t in range(half_ring + 1):
-            if t > 0:
-                while handled < min(2 * t, last + 1):
-                    ring_step(handled)
-                    handled += 1
-            arrived(t)
-            for block in blocks_at(t):
-                home = block // out_units == hid
-                j = block % out_units
-
-                @pl.when(jnp.logical_not(home))
-                def _():
-                    send_terms(j)
-
-                @pl.when(home)
-                def _():
-                    term_home[j] = terms(hid * width, j)
-
-            for block in blocks_at(t - 1) if t > 0 else []:
-                @pl.when(block // out_units == hid)
-                def _():
-                    finish(block % out_units)
-
-        for block in blocks_at(half_ring):
+        for n, (arrived, block) in enumerate(order):
+            arrived()
+
+            @pl.when(block // out_units != hid)
+            def _():
+                send_terms(block % out_units)
+
             @pl.when(block // out_units == hid)
             def _():
-                finish(block % out_units)
+                term_home[block % out_units] = terms(hid * width, block % out_units)
+
+            if n > 0:
+                finish_block(order[n - 1][1])
+        finish_block(order[-1][1])
     else:
-        for s in range(handled, last + 1):
-            ring_step(s)
-        for t in range(half_ring + 1):
-            arrived(t)
+        for arrived, _ in order:
+            arrived()
 
         def away(j, _):
             send_terms(j)
@@ -428,10 +436,12 @@
         return 0
 
     lax.fori_loop(0, groups, sent, 0)
-    for s in range(last + 1):
-        for way in range(2):
-            ring_copy(way, s).wait_send()
-            ring_mate(way, s, core).wait_send()
+    for i in range(column):
+        over_copy(i).wait_send()
+        over_mate(i, core).wait_send()
+        if i > 0:
+            up_copy(i).wait_send()
+            up_mate(i, core).wait_send()
     wown_copy().wait_send()
 
     def term_sent(j, _):
@@ -452,7 +462,7 @@
     smem = pl.BlockSpec(memory_space=pltpu.SMEM)
     hbm = pl.BlockSpec(memory_space=pl.ANY)
     dma = pltpu.SemaphoreType.DMA
-    half_ring = chips // 2
+    column = chips // 2
     return pl.pallas_call(
         functools.partial(block_kernel, chips),
         out_shape=jax.ShapeDtypeStruct((rows, width), jnp.bfloat16),
@@ -470,7 +480,7 @@
             pltpu.VMEM((out_units, rows, UNIT), jnp.float32),
             pltpu.VMEM((1, SLOTS * TILE), jnp.float32),
             dma((3,)), dma((2,)),
-        ] + [dma((groups,))] * 12 + [dma((2, 2 * half_ring - 1))] * 4 + [dma((1,))] * 2
+        ] + [dma((groups,))] * 12 + [dma((column,))] * 8 + [dma((1,))] * 2
         + [dma((out_units,))] * 2,
         compiler_params=pltpu.CompilerParams(
             collective_id=0, has_side_effects=True, vmem_limit_bytes=62 * 1024 * 1024

time: 215 us -> 236 us (1.098)
  Pallas kernels: 212 us -> 231 us
    pallas_call x1, Pallas kernels: 212 us -> 231 us  [on_device(): pl.pallas_call(functools.partial(block_kernel, chips), out_shape=jax.Shap...]
where the time goes in v3:
time: 236 us; the launch traced here: 234 us
  Pallas kernels  231 us (98%)
  local copies, waits for them, and re-layouts  2.36 us (1%)
    pallas_call x1, Pallas kernels, on_device(): pl.pallas_call(functools.partial(block_kernel, chips), out_shape=jax.Shap...  231 us

profile of v3, /device:TPU:0, one launch (start us, length us, event | category | flops | bytes accessed | tf_op | source)
XLA Modules:
  0.0 233.7 jit_solution(15369768487452696817)
XLA Ops:
  0.0 231.4 %shard_map.100 = bf16[384,1536]{1,0:T(8,128)(2,1)} custom-call(bf16[384,1536]{1,0:T(8,128)(2,1)} %q_ref.1, bf16[384,1536]{1,0:T(8,128)(2,1)} %res_ref.1, f32[1,3072]{1,0:T(1,128)} %bitcast.4, f32[1,3072]{1,0:T(1,128)} %bitcast.5, s32[16]{0:T(128)} %slot_ref.1, s32[16,27]{1,0:T(8,128)} %list_ref.1, bf16[384,1536]{1,0:T(8,128)(2,1)} %k_hbm.1, ...), custom_call_target="tpu_custom_call" | custom-call | tf_op jit(solution)/shard_map/pallas_call | solution.py:466
  231.4 2.4 %copy.12 = bf16[384,1536]{1,0:T(8,128)(2,1)} copy(bf16[384,1536]{1,0:T(8,128)(2,1)} %shard_map.100) | data formatting | bytes 2359296

commit v4 on v2

--- a/solution.py
+++ b/solution.py
@@ -14,8 +14,9 @@
 GROUP = 256
 W_CHUNK = 512
 UNIT = 384
-RING_GROUPS = (1, 2, 4, 5)
-RING_CHUNK = 2
+RING_START = 4
+RING_GROUPS = (6,)
+RING_CHUNKS = (0, 2, 5)
 MESH = pl.DeviceIdType.MESH
 
 
@@ -189,9 +190,6 @@
 
     lax.fori_loop(0, groups, send_own, 0)
     loads[2].wait()
-    for s in range(2):
-        ring_copy(0, s).start()
-        ring_copy(1, s).start()
     wown_copy().start()
 
     tiles = slot_ref.shape[0]
@@ -251,6 +249,12 @@
 
             cn_copy(g).start()
 
+        @pl.when(g == RING_START)
+        def _():
+            for s in range(2):
+                ring_copy(0, s).start()
+                ring_copy(1, s).start()
+
         @pl.when(g >= 1)
         def _():
             prior = g - 1
@@ -317,15 +321,16 @@
         def _():
             win_copy(j + 2, slot).start()
 
-        @pl.when(j == RING_CHUNK)
-        def _():
-            ring_step(len(RING_GROUPS))
+        for s, when in enumerate(RING_CHUNKS):
+            @pl.when(j == when)
+            def _():
+                ring_step(len(RING_GROUPS) + s)
 
         return 0
 
     lax.fori_loop(0, w_chunks, project, 0)
 
-    handled = len(RING_GROUPS) + 1
+    handled = len(RING_GROUPS) + len(RING_CHUNKS)
     wown_in = wout_part(chip, 1 - core, pl.ds(0, units))
 
     def arrived(t):

time: 215 us -> 184 us (0.86)
  Pallas kernels: 212 us -> 181 us
    pallas_call x1, Pallas kernels: 212 us -> 181 us  [on_device(): pl.pallas_call(functools.partial(block_kernel, chips), out_shape=jax.Shap...]
where the time goes in v4:
time: 184 us
  Pallas kernels  181 us (98%)
  local copies, waits for them, and re-layouts  2.36 us (1%)
    pallas_call x1, Pallas kernels, on_device(): pl.pallas_call(functools.partial(block_kernel, chips), out_shape=jax.Shap...  181 us

profile of v4, /device:TPU:0, one launch (start us, length us, event | category | flops | bytes accessed | tf_op | source)
XLA Modules:
  0.0 183.7 jit_solution(2846206639152937068)
XLA Ops:
  0.0 181.3 %shard_map.100 = bf16[384,1536]{1,0:T(8,128)(2,1)} custom-call(bf16[384,1536]{1,0:T(8,128)(2,1)} %q_ref.1, bf16[384,1536]{1,0:T(8,128)(2,1)} %res_ref.1, f32[1,3072]{1,0:T(1,128)} %bitcast.4, f32[1,3072]{1,0:T(1,128)} %bitcast.5, s32[16]{0:T(128)} %slot_ref.1, s32[16,27]{1,0:T(8,128)} %list_ref.1, bf16[384,1536]{1,0:T(8,128)(2,1)} %k_hbm.1, ...), custom_call_target="tpu_custom_call" | custom-call | tf_op jit(solution)/shard_map/pallas_call | solution.py:461
  181.4 2.4 %copy.12 = bf16[384,1536]{1,0:T(8,128)(2,1)} copy(bf16[384,1536]{1,0:T(8,128)(2,1)} %shard_map.100) | data formatting | bytes 2359296

commit v5 on v4

--- a/solution.py
+++ b/solution.py
@@ -17,6 +17,7 @@
 RING_START = 4
 RING_GROUPS = (6,)
 RING_CHUNKS = (0, 2, 5)
+EXP_SCALE = math.log2(math.e) / math.sqrt(HEAD_DIM)
 MESH = pl.DeviceIdType.MESH
 
 
@@ -24,7 +25,7 @@
     chips,
     q_ref, res_ref, scale_ref, gate_ref, slot_ref, list_ref, k_hbm, v_hbm, win_hbm, wout_hbm,
     out_ref,
-    kv, wout, win, comb, normed, hidden, term_out, term_in, term_home, bias_ref,
+    kv, wout, win, comb, normed, hidden, term_out, term_in, term_home,
     local_sem, win_sem, near_s, near_r, far_s, far_r, own_s, own_r, cn_s, cn_r, cf_s, cf_r,
     x_s, x_r, ring_s, ring_r, cring_s, cring_r, wown_s, wown_r, term_s, term_r,
 ):
@@ -192,6 +193,7 @@
     loads[2].wait()
     wown_copy().start()
 
+    masks = []
     tiles = slot_ref.shape[0]
     own_tile = slot_ref[seq]
     for i in range(SLOTS):
@@ -201,9 +203,7 @@
         hits = jnp.int32(0)
         for j in range(list_ref.shape[1]):
             hits = hits + (list_ref[own_tile, j] == tile).astype(jnp.int32)
-        bias_ref[:, i * TILE : (i + 1) * TILE] = jnp.where(
-            jnp.full((1, TILE), hits * inside) > 0, 0.0, -jnp.inf
-        ).astype(jnp.float32)
+        masks.append(jnp.where(hits * inside > 0, jnp.float32(0.0), jnp.float32(-jnp.inf)))
 
     @pl.when(jnp.logical_not(has_far))
     def _():
@@ -214,16 +214,29 @@
     def attend(g):
         def head(h, _):
             lanes = pl.ds(pl.multiple_of(g * GROUP + h * HEAD_DIM, HEAD_DIM), HEAD_DIM)
-            scores = lax.dot_general(
-                q_ref[:, lanes], kv[0, :, lanes], (((1,), (1,)), ((), ())),
-                preferred_element_type=jnp.float32,
+            query = q_ref[:, lanes]
+            scores = []
+            for i in range(0, SLOTS, 2):
+                pair = lax.dot_general(
+                    query, kv[0, i * TILE : (i + 2) * TILE, lanes], (((1,), (1,)), ((), ())),
+                    preferred_element_type=jnp.float32,
+                )
+                scores += [pair[:, :TILE], pair[:, TILE:]]
+            row_max = functools.reduce(
+                jnp.maximum,
+                [jnp.max(s, axis=-1, keepdims=True) + b for s, b in zip(scores, masks)],
             )
-            scores = scores * (1.0 / math.sqrt(HEAD_DIM)) + bias_ref[...]
-            probs = jnp.exp(scores - jnp.max(scores, axis=-1, keepdims=True))
-            total = jnp.sum(probs, axis=-1, keepdims=True)
-            mixed = jnp.dot(
-                probs.astype(jnp.bfloat16), kv[1, :, lanes], preferred_element_type=jnp.float32
-            )
+            total = mixed = 0.0
+            for i in range(0, SLOTS, 2):
+                halves = []
+                for k in (i, i + 1):
+                    probs = jnp.exp2((scores[k] - (row_max - masks[k])) * EXP_SCALE)
+                    total = total + jnp.sum(probs, axis=-1, keepdims=True)
+                    halves.append(probs.astype(jnp.bfloat16))
+                mixed = mixed + jnp.dot(
+                    jnp.concatenate(halves, axis=1), kv[1, i * TILE : (i + 2) * TILE, lanes],
+                    preferred_element_type=jnp.float32,
+                )
             attn = (mixed / total).astype(jnp.bfloat16)
             summed = res_ref[:, lanes].astype(jnp.float32) + attn.astype(jnp.float32)
             lanes_to = pl.ds(
@@ -473,7 +486,6 @@
             pltpu.VMEM((out_units, rows, UNIT), jnp.bfloat16),
             pltpu.VMEM((out_units, rows, UNIT), jnp.bfloat16),
             pltpu.VMEM((out_units, rows, UNIT), jnp.float32),
-            pltpu.VMEM((1, SLOTS * TILE), jnp.float32),
             dma((3,)), dma((2,)),
         ] + [dma((groups,))] * 12 + [dma((2, 2 * half_ring - 1))] * 4 + [dma((1,))] * 2
         + [dma((out_units,))] * 2,

time: 184 us -> 182 us (0.989)
  Pallas kernels: 181 us -> 179 us
    pallas_call x1, Pallas kernels: 181 us -> 179 us  [on_device(): pl.pallas_call(functools.partial(block_kernel, chips), out_shape=jax.Shap...]
where the time goes in v5:
time: 182 us; the launch traced here: 181 us
  Pallas kernels  179 us (98%)
  local copies, waits for them, and re-layouts  2.36 us (1%)
    pallas_call x1, Pallas kernels, on_device(): pl.pallas_call(functools.partial(block_kernel, chips), out_shape=jax.Shap...  179 us

profile of v5, /device:TPU:0, one launch (start us, length us, event | category | flops | bytes accessed | tf_op | source)
XLA Modules:
  0.0 181.4 jit_solution(15579878760509548192)
XLA Ops:
  0.0 179.1 %shard_map.100 = bf16[384,1536]{1,0:T(8,128)(2,1)} custom-call(bf16[384,1536]{1,0:T(8,128)(2,1)} %q_ref.1, bf16[384,1536]{1,0:T(8,128)(2,1)} %res_ref.1, f32[1,3072]{1,0:T(1,128)} %bitcast.4, f32[1,3072]{1,0:T(1,128)} %bitcast.5, s32[16]{0:T(128)} %slot_ref.1, s32[16,27]{1,0:T(8,128)} %list_ref.1, bf16[384,1536]{1,0:T(8,128)(2,1)} %k_hbm.1, ...), custom_call_target="tpu_custom_call" | custom-call | tf_op jit(solution)/shard_map/pallas_call | solution.py:474
  179.1 2.4 %copy.12 = bf16[384,1536]{1,0:T(8,128)(2,1)} copy(bf16[384,1536]{1,0:T(8,128)(2,1)} %shard_map.100) | data formatting | bytes 2359296

commit v6 on v5

--- a/solution.py
+++ b/solution.py
@@ -14,9 +14,9 @@
 GROUP = 256
 W_CHUNK = 512
 UNIT = 384
-RING_START = 4
-RING_GROUPS = (6,)
-RING_CHUNKS = (0, 2, 5)
+RING_START = 2
+RING_GROUPS = (5, 6)
+RING_CHUNKS = (0, 2, 4, 5)
 EXP_SCALE = math.log2(math.e) / math.sqrt(HEAD_DIM)
 MESH = pl.DeviceIdType.MESH
 

time: 182 us -> 195 us (1.071)
  Pallas kernels: 179 us -> 192 us
    pallas_call x1, Pallas kernels: 179 us -> 192 us  [on_device(): pl.pallas_call(functools.partial(block_kernel, chips), out_shape=jax.Shap...]
where the time goes in v6:
time: 195 us; the launch traced here: 194 us
  Pallas kernels  192 us (98%)
  local copies, waits for them, and re-layouts  2.36 us (1%)
    pallas_call x1, Pallas kernels, on_device(): pl.pallas_call(functools.partial(block_kernel, chips), out_shape=jax.Shap...  192 us

profile of v6, /device:TPU:0, one launch (start us, length us, event | category | flops | bytes accessed | tf_op | source)
XLA Modules:
  0.0 194.0 jit_solution(12333609190832746975)
XLA Ops:
  0.0 191.6 %shard_map.100 = bf16[384,1536]{1,0:T(8,128)(2,1)} custom-call(bf16[384,1536]{1,0:T(8,128)(2,1)} %q_ref.1, bf16[384,1536]{1,0:T(8,128)(2,1)} %res_ref.1, f32[1,3072]{1,0:T(1,128)} %bitcast.4, f32[1,3072]{1,0:T(1,128)} %bitcast.5, s32[16]{0:T(128)} %slot_ref.1, s32[16,27]{1,0:T(8,128)} %list_ref.1, bf16[384,1536]{1,0:T(8,128)(2,1)} %k_hbm.1, ...), custom_call_target="tpu_custom_call" | custom-call | tf_op jit(solution)/shard_map/pallas_call | solution.py:474
  191.6 2.4 %copy.12 = bf16[384,1536]{1,0:T(8,128)(2,1)} copy(bf16[384,1536]{1,0:T(8,128)(2,1)} %shard_map.100) | data formatting | bytes 2359296
